TPU v7x, 32 devices: a whole 2x2x4 slice. The times are simulated.
32 devices in a mesh: groups: 2 (over y), row: 4 (over z), col: 4 (over x, core).
Axes of the slice: x: 2, y: 2, z: 4, core: 2. Of those that a mesh axis runs over, the one named last changes fastest.
Arguments:
- forward: bfloat16 [32768, 1024], P(('groups', 'row', 'col')), parts along dimension 0, may hold values from 0.049804688 to 1
- adjoint: bfloat16 [32768, 1024], P(('groups', 'col', 'row')), parts along dimension 0, may hold values from 0.049804688 to 1
- emission: bfloat16 [16384, 256], P(('col', 'row')), may hold values from 0.0099487305 to 1
- emit_index: int32 [2048], P('groups'), parts along dimension 0, may hold values from 0 to 255
- transition: bfloat16 [16384, 16384], P('row', 'col'), may hold values from 0.02 to 30
Outputs:
- updated: bfloat16 [32768, 16384], P(('groups', 'row'), 'col'), parts along dimension 0
There are 2 independent parts, one for each index of `groups`. A program takes and returns all parts, laid end to end along the dimension named above; an argument that names none is the same for every part. Nothing has to cross between parts.
All inputs are finite; a program needn't handle non-finite values.
Results may differ from a plain program's by a relative error of at most 0.0034.
Values may be sent and summed in bfloat16 or wider, within the bound.
A program may use at most 320 MiB of HBM per device.

v0:
```python
import jax
import jax.numpy as jnp
from jax import lax
from jax.sharding import PartitionSpec as P

STATES = 16384


def body(forward, adjoint, emission, emit_index, transition):
    source_msgs = lax.all_gather(forward, "col", axis=0, tiled=True)
    classes = emission.shape[1]
    one_hot = (emit_index[None, :] == lax.iota(jnp.int32, classes)[:, None]).astype(jnp.bfloat16)
    pieces = lax.all_gather((adjoint, emission), "row", axis=0, tiled=True)
    looked = jnp.dot(pieces[1], one_hot, preferred_element_type=jnp.float32)
    counts = lax.dot_general(
        source_msgs,
        (pieces[0].astype(jnp.float32) * looked).astype(jnp.bfloat16),
        (((1,), (1,)), ((), ())),
        preferred_element_type=jnp.float32,
    )
    scaled = counts * transition.astype(jnp.float32)
    partial_total = jnp.sum(scaled, axis=1)
    total = lax.psum(partial_total, "col")
    return (scaled * (STATES / total)[:, None]).astype(jnp.bfloat16)


def solution(mesh):
    return jax.shard_map(
        body,
        mesh=mesh,
        in_specs=(
            P(("groups", "row", "col"), None),
            P(("groups", "col", "row"), None),
            P(("col", "row"), None),
            P("groups"),
            P("row", "col"),
        ),
        out_specs=P(("groups", "row"), "col"),
        check_vma=False,
    )
```

profile of v0, /device:TPU:0, one launch (start us, length us, event | category | flops | bytes accessed | tf_op | source)
XLA Modules:
  0.0 417.8 jit_solution(8021108147237351209)
XLA Ops:
  6.5 0.0 all-gather.6.cloned.1.call-start
  6.5 0.7 all-gather.6.cloned.1.call-update
  7.3 0.0 all-gather.4.cloned.1.call-start
  7.3 0.7 all-gather.4.cloned.1.call-update
  8.0 0.0 all-gather.8.cloned.1.call-start
  8.1 0.7 all-gather.8.cloned.1.call-update
  8.7 0.0 copy-start
  8.8 44.2 %copy.6 = bf16[4096,4096]{0,1:T(8,128)(2,1)} copy(bf16[4096,4096]{1,0:T(8,128)(2,1)} %param.9) | data formatting | bytes 67108864 | tf_op args[4]
  52.9 4.7 %all-gather.6.cloned.1.call-done = bf16[4096,256]{1,0:T(8,128)(2,1)} async-done(((bf16[1024,256]{1,0:T(8,128)(2,1)}), bf16[4096,256]{1,0:T(8,128)(2,1)}) %all-gather.6.cloned.1.call-update) | async-done | bytes 2097168 | tf_op jit(solution)/shard_map/all_gather | solution.py:13
  57.6 149.9 %all-gather.4.cloned.1.call-done = bf16[4096,1024]{1,0:T(8,128)(2,1)} async-done(((bf16[1024,1024]{1,0:T(8,128)(2,1)}), bf16[4096,1024]{1,0:T(8,128)(2,1)}) %all-gather.4.cloned.1.call-update) | async-done | bytes 8388624 | tf_op jit(solution)/shard_map/all_gather | solution.py:13
  207.5 0.0 copy-done
  207.6 10.7 %fusion.1.clone.1.clone.4 = bf16[4096,1024]{1,0:T(8,128)(2,1)} fusion(bf16[4096,1024]{1,0:T(8,128)(2,1)} %all-gather.4.cloned.1.call-done, bf16[4096,256]{1,0:T(8,128)(2,1)} %all-gather.6.cloned.1.call-done, s32[1024]{0:T(1024)S(1)} %copy-done), kind=kOutput, calls=%fused_computation.4.clone.clone.clone.clone.clone.1 | convolution fusion | flops 2160328704 | bytes 18878464 | tf_op jit(solution)/shard_map/dot_general | solution.py:14
  218.2 47.4 %all-gather.8.cloned.1.call-done = bf16[4096,1024]{1,0:T(8,128)(2,1)} async-done(((bf16[1024,1024]{1,0:T(8,128)(2,1)}), bf16[4096,1024]{1,0:T(8,128)(2,1)}) %all-gather.8.cloned.1.call-update) | async-done | bytes 8388624 | tf_op jit(solution)/shard_map/all_gather | solution.py:10
  265.7 48.1 %fusion = (f32[4096]{0:T(1024)S(1)}, f32[4096,4096]{1,0:T(8,128)}) fusion(bf16[4096,4096]{0,1:T(8,128)(2,1)} %copy.6, bf16[4096,1024]{1,0:T(8,128)(2,1)} %all-gather.8.cloned.1.call-done, bf16[4096,1024]{1,0:T(8,128)(2,1)} %fusion.1.clone.1.clone.4), kind=kOutput, calls=%fused_computation.2 | convolution fusion | flops 34410065920 | bytes 117456896 | tf_op jit(solution)/shard_map/dot_general | solution.py:15
  313.7 10.2 %psum.7 = f32[4096]{0:T(1024)S(1)} all-reduce(f32[4096]{0:T(1024)S(1)} %get-tuple-element.5), channel_id=1, replica_groups=mesh['groups'=2,'row'=4,'col'=4] {'col'}, use_global_device_ids=true, to_apply=%region_1.0 | all-reduce | flops 4096 | bytes 32768 | tf_op jit(solution)/shard_map/psum | solution.py:23
  324.0 43.2 %multiply_convert_fusion = bf16[4096,4096]{0,1:T(8,128)(2,1)} fusion(bf16[4096,4096]{0,1:T(8,128)(2,1)} %copy.6, f32[4096,4096]{1,0:T(8,128)} %get-tuple-element.6, f32[4096]{0:T(1024)S(1)} %broadcast_divide_fusion), kind=kLoop, calls=%fused_computation.1 | loop fusion | flops 67108864 | bytes 134234112 | tf_op jit(solution)/shard_map/convert_element_type | solution.py:24
  367.2 44.1 %copy.7 = bf16[4096,4096]{1,0:T(8,128)(2,1)} copy(bf16[4096,4096]{0,1:T(8,128)(2,1)} %multiply_convert_fusion) | data formatting | bytes 67108864 | tf_op jit(solution)/shard_map/convert_element_type | solution.py:24
  (1 shorter events, 0.0 us)
Async XLA Ops:
  6.5 51.1 %all-gather.6.cloned.1.call-start = ((), (), s32[]{:S(2)}) async-start(), calls=%async_computation.1 | async-start | bytes 2621440 | tf_op jit(solution)/shard_map/all_gather | solution.py:13
  7.3 200.3 %all-gather.4.cloned.1.call-start = ((), (), s32[]{:S(2)}) async-start(), calls=%async_computation | async-start | bytes 10485760 | tf_op jit(solution)/shard_map/all_gather | solution.py:13
  8.0 257.7 %all-gather.8.cloned.1.call-start = ((), (), s32[]{:S(2)}) async-start(), calls=%async_computation.2 | async-start | bytes 10485760 | tf_op jit(solution)/shard_map/all_gather | solution.py:10
  8.7 198.8 %copy-start = (s32[1024]{0:T(1024)S(1)}, s32[1024]{0:T(1024)}, u32[]{:S(2)}) copy-start(s32[1024]{0:T(1024)} %param.8) | copy-start | bytes 12292
Sparse Core Ops, SparseCore 0:
  8.9 48.6 all-gather.5
  59.2 148.3 all-gather.3
  209.1 56.4 all-gather.7
where the time goes:
time: 420 us; the launch traced here: 418 us
  waiting for transfers between devices  204 us (49%)
  local copies, waits for them, and re-layouts  88.3 us (21%)
  matrix products  58.8 us (14%)
  other arithmetic  43.2 us (10%)
  between operations  13.1 us (3%)
  blocking collectives  10.2 us (2%)
    all_gather x2, waiting for transfers between devices, body(): pieces = lax.all_gather((adjoint, emission), 'row', axis=0, tiled=True)  155 us
    dot_general x1, matrix products, body(): lax.dot_general(source_msgs, (pieces[0].astype(jnp.float32) * looked).ast...  48.1 us
    all_gather x1, waiting for transfers between devices, body(): source_msgs = lax.all_gather(forward, 'col', axis=0, tiled=True)  47.4 us
    unnamed x3, local copies, waits for them, and re-layouts  44.2 us
    convert_element_type x1, local copies, waits for them, and re-layouts, body(): return (scaled * (STATES / total)[:, None]).astype(jnp.bfloat16)  44.1 us
    convert_element_type x1, other arithmetic, body(): return (scaled * (STATES / total)[:, None]).astype(jnp.bfloat16)  43.2 us
    dot_general x1, matrix products, body(): looked = jnp.dot(pieces[1], one_hot, preferred_element_type=jnp.float32)  10.7 us
    psum x1, blocking collectives, body(): total = lax.psum(partial_total, 'col')  10.2 us
  transfers between devices with their start and end apart: 3, of which 3 were waited for; matrix products, arithmetic and copies ran while one was open for 13% of the time, Pallas kernels for 0%

commit v1 on v0

v1 whole, which is shorter than its diff:
```python
import functools

import jax
import jax.numpy as jnp
from jax import lax
from jax.experimental import pallas as pl
from jax.experimental.pallas import tpu as pltpu
from jax.sharding import PartitionSpec as P

CHUNK = 256
ROWS = 512
MESH = pl.DeviceIdType.MESH


def kernel(n, m, states, idx_ref, em_ref, adj_ref, fwd_ref, trans_ref,
           scaled_ref, factor_ref,
           w, f, tbuf, obuf, acc, tot,
           w_recv, w_right, w_left, f_recv, f_right, f_left,
           t_sem, o_sem, tot_send, tot_recv, load_sem):
    groups = lax.axis_index("groups")
    p = lax.axis_index("row")
    c = lax.axis_index("col")
    shard = adj_ref.shape[0]
    chunks = shard // CHUNK
    rows = f.shape[0]
    symbols = em_ref.shape[1]
    positions = adj_ref.shape[1]

    def row_dev(q):
        return (groups, q, c)

    def col_dev(q):
        return (groups, p, q)

    def w_copy(i, sem, dev):
        return pltpu.make_async_remote_copy(
            src_ref=w.at[i], dst_ref=w.at[i], send_sem=sem.at[i], recv_sem=w_recv.at[i],
            device_id=row_dev(dev), device_id_type=MESH)

    def f_slice(i):
        return f.at[pl.ds(pl.multiple_of(i * CHUNK, CHUNK), CHUNK)]

    def f_copy(i, sem, dev):
        return pltpu.make_async_remote_copy(
            src_ref=f_slice(i), dst_ref=f_slice(i), send_sem=sem.at[i], recv_sem=f_recv.at[i],
            device_id=col_dev(dev), device_id_type=MESH)

    barrier = pltpu.get_barrier_semaphore()

    @pl.when(p > 0)
    def _():
        pl.semaphore_signal(barrier, inc=1, device_id=row_dev(p - 1), device_id_type=MESH)

    @pl.when(p < n - 1)
    def _():
        pl.semaphore_signal(barrier, inc=1, device_id=row_dev(p + 1), device_id_type=MESH)

    for step in range(1, m):
        pl.semaphore_signal(barrier, inc=1, device_id=col_dev(lax.rem(c + step, m)), device_id_type=MESH)

    load = pltpu.make_async_copy(fwd_ref, f.at[pl.ds(pl.multiple_of(c * shard, CHUNK), shard)], load_sem)
    load.start()

    def own_block(k):
        at = pl.ds(pl.multiple_of(k * CHUNK, CHUNK), CHUNK)
        one_hot = jnp.where(
            idx_ref[...] == lax.broadcasted_iota(jnp.int32, (symbols, positions), 0), 1.0, 0.0
        ).astype(jnp.bfloat16)
        looked = jnp.dot(em_ref[at, :], one_hot, preferred_element_type=jnp.float32)
        block = adj_ref[at, :].astype(jnp.float32) * looked
        w[p * chunks + k] = block.T.astype(jnp.bfloat16)

    own_block(0)
    pl.semaphore_wait(barrier, jnp.where(p > 0, 1, 0) + jnp.where(p < n - 1, 1, 0) + (m - 1))

    def send_own(k, _):
        @pl.when(k > 0)
        def _():
            own_block(k)

        i = p * chunks + k

        @pl.when(p > 0)
        def _():
            w_copy(i, w_left, p - 1).start()

        @pl.when(p < n - 1)
        def _():
            w_copy(i, w_right, p + 1).start()

        @pl.when(k == 0)
        def _():
            load.wait()

            def send_forward(kf, _):
                j = c * chunks + kf

                @pl.when(c > 0)
                def _():
                    f_copy(j, f_left, c - 1).start()

                @pl.when(c < m - 1)
                def _():
                    f_copy(j, f_right, c + 1).start()

                return 0

            lax.fori_loop(0, chunks, send_forward, 0)

        return 0

    lax.fori_loop(0, chunks, send_own, 0)

    def w_arrive(slot, k):
        i = slot * chunks + k

        @pl.when((slot >= 0) & (slot < n))
        def _():
            w_copy(i, w_left, p).wait_recv()

            @pl.when((slot < p) & (p < n - 1))
            def _():
                w_copy(i, w_right, p + 1).start()

            @pl.when((slot > p) & (p > 0))
            def _():
                w_copy(i, w_left, p - 1).start()

    def f_arrive(slot, k):
        i = slot * chunks + k

        @pl.when((slot >= 0) & (slot < m))
        def _():
            f_copy(i, f_left, c).wait_recv()

            @pl.when((slot < c) & (c < m - 1))
            def _():
                f_copy(i, f_right, c + 1).start()

            @pl.when((slot > c) & (c > 0))
            def _():
                f_copy(i, f_left, c - 1).start()

    def gather(step, _):
        d = 1 + step // chunks
        k = lax.rem(step, chunks)
        f_arrive(c - d, k)
        f_arrive(c + d, k)

        @pl.when(d == m - 1)
        def _():
            w_arrive(p - 1, k)
            w_arrive(p + 1, k)

        return 0

    acc[...] = jnp.zeros_like(acc)
    lax.fori_loop(0, (m - 1) * chunks, gather, 0)

    both = jnp.minimum(p, n - 1 - p)

    def slot_of(o):
        near = (o + 1) // 2
        near_slot = jnp.where(lax.rem(o, 2) == 1, p - near, p + near)
        far = o - both
        far_slot = jnp.where(p > n - 1 - p, p - far, p + far)
        return jnp.where(o <= 2 * both, near_slot, far_slot)

    def columns(q):
        i = slot_of(q // chunks) * chunks + lax.rem(q, chunks)
        return pl.ds(pl.multiple_of(i * CHUNK, CHUNK), CHUNK)

    def t_copy(q):
        b = lax.rem(q, 2)
        return pltpu.make_async_copy(trans_ref.at[:, columns(q)], tbuf.at[b], t_sem.at[b])

    def o_copy(q):
        b = lax.rem(q, 2)
        return pltpu.make_async_copy(obuf.at[b], scaled_ref.at[:, columns(q)], o_sem.at[b])

    t_copy(0).start()

    def block(q, _):
        slot = slot_of(q // chunks)
        k = lax.rem(q, chunks)
        b = lax.rem(q, 2)

        @pl.when(q + 1 < n * chunks)
        def _():
            t_copy(q + 1).start()

        @pl.when(jnp.abs(slot - p) > 1)
        def _():
            w_arrive(slot, k)

        @pl.when(q >= 2)
        def _():
            o_copy(q - 2).wait()

        t_copy(q).wait()
        i = slot * chunks + k

        def tile(r, _):
            at = pl.ds(pl.multiple_of(r * ROWS, ROWS), ROWS)
            counts = jnp.dot(f[at, :], w[i], preferred_element_type=jnp.float32)
            scaled = counts * tbuf[b, at, :].astype(jnp.float32)
            obuf[b, at, :] = scaled.astype(jnp.bfloat16)
            part = scaled[:, :128]
            for g in range(1, CHUNK // 128):
                part = part + scaled[:, g * 128:(g + 1) * 128]
            acc[at, :] += part
            return 0

        lax.fori_loop(0, rows // ROWS, tile, 0)
        o_copy(q).start()
        return 0

    lax.fori_loop(0, n * chunks, block, 0)

    def reduce(r, _):
        at = pl.ds(pl.multiple_of(r * ROWS, ROWS), ROWS)
        tot[c, :, at] = jnp.sum(acc[at, :].T, axis=0, keepdims=True)
        return 0

    lax.fori_loop(0, rows // ROWS, reduce, 0)

    def tot_copy(src, send, dev):
        return pltpu.make_async_remote_copy(
            src_ref=tot.at[src], dst_ref=tot.at[src], send_sem=tot_send.at[send], recv_sem=tot_recv.at[src],
            device_id=col_dev(dev), device_id_type=MESH)

    for step in range(1, m):
        tot_copy(c, step, lax.rem(c + step, m)).start()
    o_copy(n * chunks - 2).wait()
    o_copy(n * chunks - 1).wait()
    for step in range(1, m):
        tot_copy(lax.rem(c + step, m), step, c).wait_recv()
    factor_ref[...] = states / jnp.sum(tot[...], axis=0)
    for step in range(1, m):
        tot_copy(c, step, lax.rem(c + step, m)).wait_send()

    def sent(i, _):
        slot = i // chunks

        @pl.when((slot >= p) & (p > 0))
        def _():
            w_copy(i, w_left, p - 1).wait_send()

        @pl.when((slot <= p) & (p < n - 1))
        def _():
            w_copy(i, w_right, p + 1).wait_send()

        return 0

    lax.fori_loop(0, n * chunks, sent, 0)

    def f_sent(i, _):
        slot = i // chunks

        @pl.when((slot >= c) & (c > 0))
        def _():
            f_copy(i, f_left, c - 1).wait_send()

        @pl.when((slot <= c) & (c < m - 1))
        def _():
            f_copy(i, f_right, c + 1).wait_send()

        return 0

    lax.fori_loop(0, m * chunks, f_sent, 0)


def fused(n, m, forward, adjoint, emission, emit_index, transition):
    rows, cols = transition.shape
    shard, positions = forward.shape
    chunks = shard // CHUNK
    vmem = pl.BlockSpec(memory_space=pltpu.VMEM)
    anywhere = pl.BlockSpec(memory_space=pl.ANY)
    dma = pltpu.SemaphoreType.DMA
    scaled, factor = pl.pallas_call(
        functools.partial(kernel, n, m, float(cols * m)),
        out_shape=(
            jax.ShapeDtypeStruct((rows, cols), jnp.bfloat16),
            jax.ShapeDtypeStruct((1, rows), jnp.float32),
        ),
        in_specs=[vmem, vmem, vmem, anywhere, anywhere],
        out_specs=(anywhere, vmem),
        scratch_shapes=[
            pltpu.VMEM((n * chunks, positions, CHUNK), jnp.bfloat16),
            pltpu.VMEM((rows, positions), jnp.bfloat16),
            pltpu.VMEM((2, rows, CHUNK), jnp.bfloat16),
            pltpu.VMEM((2, rows, CHUNK), jnp.bfloat16),
            pltpu.VMEM((rows, 128), jnp.float32),
            pltpu.VMEM((m, 1, rows), jnp.float32),
            dma((n * chunks,)), dma((n * chunks,)), dma((n * chunks,)),
            dma((m * chunks,)), dma((m * chunks,)), dma((m * chunks,)),
            dma((2,)), dma((2,)), dma((m,)), dma((m,)), dma,
        ],
        compiler_params=pltpu.CompilerParams(
            collective_id=0, has_side_effects=True, vmem_limit_bytes=48 * 1024 * 1024),
        cost_estimate=pl.CostEstimate(
            flops=2 * rows * cols * positions, bytes_accessed=4 * rows * cols, transcendentals=0),
        name="counts_gather",
    )(emit_index.reshape(1, -1), emission, adjoint, forward, transition)
    return (scaled.astype(jnp.float32) * factor.reshape(rows, 1)).astype(jnp.bfloat16)


def plain(m, forward, adjoint, emission, emit_index, transition):
    symbols = emission.shape[1]
    one_hot = (emit_index[None, :] == lax.iota(jnp.int32, symbols)[:, None]).astype(jnp.bfloat16)
    looked = jnp.dot(emission, one_hot, preferred_element_type=jnp.float32)
    weighted = (adjoint.astype(jnp.float32) * looked).astype(jnp.bfloat16)
    sources = lax.all_gather(forward, "col", axis=0, tiled=True)
    targets = lax.all_gather(weighted, "row", axis=0, tiled=True)
    counts = lax.dot_general(sources, targets, (((1,), (1,)), ((), ())), preferred_element_type=jnp.float32)
    scaled = counts * transition.astype(jnp.float32)
    total = lax.psum(jnp.sum(scaled, axis=1), "col")
    return (scaled * (m * transition.shape[1] / total)[:, None]).astype(jnp.bfloat16)


def solution(mesh):
    n, m = mesh.shape["row"], mesh.shape["col"]

    def body(forward, adjoint, emission, emit_index, transition):
        args = (forward, adjoint, emission, emit_index, transition)
        if n > 2 and m > 1 and forward.shape[0] % CHUNK == 0:
            return fused(n, m, *args)
        return plain(m, *args)

    return jax.shard_map(
        body,
        mesh=mesh,
        in_specs=(
            P(("groups", "row", "col"), None),
            P(("groups", "col", "row"), None),
            P(("col", "row"), None),
            P("groups"),
            P("row", "col"),
        ),
        out_specs=P(("groups", "row"), "col"),
        check_vma=False,
    )
```

time: 420 us -> 181 us (0.43)
  waiting for transfers between devices: 204 us -> 0 us
  Pallas kernels: 0 us -> 153 us
  local copies, waits for them, and re-layouts: 88.3 us -> 4.91 us
  matrix products: 58.8 us -> 0 us
  other arithmetic: 43.2 us -> 23.1 us
  between operations: 13.1 us -> 0.01 us
  blocking collectives: 10.2 us -> 0 us
    all_gather x3 -> x0, waiting for transfers between devices: 202 us -> none  [the longest x2 155 us: body(): pieces = lax.all_gather((adjoint, emission), 'row', axis=0, tiled=True)]
    pallas_call x0 -> x1, Pallas kernels: none -> 153 us  [fused(): pl.pallas_call(functools.partial(kernel, n, m, float(cols * m)), out_shap...]
    dot_general x2 -> x0, matrix products: 58.8 us -> none  [the longest x1 48.1 us: body(): lax.dot_general(source_msgs, (pieces[0].astype(jnp.float32) * looked).ast...]
    convert_element_type x1 -> x0, local copies, waits for them, and re-layouts: 44.1 us -> none  [body(): return (scaled * (STATES / total)[:, None]).astype(jnp.bfloat16)]
    unnamed x3 -> x8, local copies, waits for them, and re-layouts: 44.2 us -> 4.91 us
    convert_element_type x1, other arithmetic: 43.2 us -> 23.1 us  [fused(): (scaled.astype(jnp.float32) * factor.reshape(rows, 1)).astype(jnp.bfloat16)]
    psum x1 -> x0, blocking collectives: 10.2 us -> none  [body(): total = lax.psum(partial_total, 'col')]
  transfers between devices with their start and end apart: 3 -> 0, of which waited for: 3 -> 0; matrix products, arithmetic and copies ran while one was open for 13% -> 0% of each run, Pallas kernels for 0% -> 0%
where the time goes in v1:
time: 181 us
  Pallas kernels  153 us (85%)
  other arithmetic  23.1 us (13%)
  local copies, waits for them, and re-layouts  4.91 us (3%)
    pallas_call x1, Pallas kernels, fused(): pl.pallas_call(functools.partial(kernel, n, m, float(cols * m)), out_shap...  153 us
    convert_element_type x1, other arithmetic, fused(): (scaled.astype(jnp.float32) * factor.reshape(rows, 1)).astype(jnp.bfloat16)  23.1 us
    unnamed x8, local copies, waits for them, and re-layouts  4.91 us

profile of v1, /device:TPU:0, one launch (start us, length us, event | category | flops | bytes accessed | tf_op | source)
XLA Modules:
  0.0 180.7 jit_solution(5167727141301518909)
XLA Ops:
  0.0 0.0 copy-start
  0.0 1.6 copy-done
  1.6 0.0 copy-start.1
  1.6 1.6 copy-done.1
  3.2 0.0 copy-start.2
  3.2 1.0 copy-done.2
  4.2 0.0 copy-start.3
  4.2 0.7 copy-done.3
  4.9 152.7 %counts_gather.1 = (bf16[4096,4096]{1,0:T(8,128)(2,1)}, f32[1,4096]{1,0:T(1,128)S(1)}) custom-call(s32[1,1024]{1,0:T(1,128)S(1)} %bitcast.3, bf16[1024,256]{1,0:T(8,128)(2,1)S(1)} %copy-done.2, bf16[1024,1024]{1,0:T(8,128)(2,1)S(1)} %copy-done, bf16[1024,1024]{1,0:T(8,128)(2,1)S(1)} %copy-done.1, bf16[4096,4096]{1,0:T(8,128)(2,1)} %trans_ref.1), custom_call_target="tpu_custom_call" | custom-call | flops 34359738368 | bytes 67108864 | tf_op jit(solution)/shard_map/counts_gather/pallas_call | solution.py:280
  157.6 23.1 %multiply_convert_fusion = bf16[4096,4096]{1,0:T(8,128)(2,1)} fusion(bf16[4096,4096]{1,0:T(8,128)(2,1)} %get-tuple-element.7, f32[4096]{0:T(1024)S(1)} %bitcast.2), kind=kLoop, calls=%fused_computation | loop fusion | flops 50331648 | bytes 67125248 | tf_op jit(solution)/shard_map/convert_element_type | solution.py:305
Async XLA Ops:
  0.0 1.6 copy-start
  1.6 1.6 copy-start.1
  3.2 1.0 copy-start.2
  4.2 0.7 copy-start.3

commit v2 on v1

--- a/solution.py
+++ b/solution.py
@@ -14,9 +14,9 @@
 
 def kernel(n, m, states, idx_ref, em_ref, adj_ref, fwd_ref, trans_ref,
            scaled_ref, factor_ref,
-           w, f, tbuf, obuf, acc, tot,
+           w, f, abuf, ebuf, tbuf, acc, tot,
            w_recv, w_right, w_left, f_recv, f_right, f_left,
-           t_sem, o_sem, tot_send, tot_recv, load_sem):
+           t_sem, a_sem, e_sem, tot_send, tot_recv, load_sem):
     groups = lax.axis_index("groups")
     p = lax.axis_index("row")
     c = lax.axis_index("col")
@@ -58,19 +58,36 @@
     for step in range(1, m):
         pl.semaphore_signal(barrier, inc=1, device_id=col_dev(lax.rem(c + step, m)), device_id_type=MESH)
 
+    def own_loads(k):
+        b = lax.rem(k, 2)
+        at = pl.ds(pl.multiple_of(k * CHUNK, CHUNK), CHUNK)
+        return (pltpu.make_async_copy(adj_ref.at[at], abuf.at[b], a_sem.at[b]),
+                pltpu.make_async_copy(em_ref.at[at], ebuf.at[b], e_sem.at[b]))
+
+    def start_loads(k):
+        for copy in own_loads(k):
+            copy.start()
+
+    start_loads(0)
     load = pltpu.make_async_copy(fwd_ref, f.at[pl.ds(pl.multiple_of(c * shard, CHUNK), shard)], load_sem)
     load.start()
 
     def own_block(k):
-        at = pl.ds(pl.multiple_of(k * CHUNK, CHUNK), CHUNK)
+        @pl.when(k + 1 < chunks)
+        def _():
+            start_loads(k + 1)
+
+        for copy in own_loads(k):
+            copy.wait()
+        b = lax.rem(k, 2)
         one_hot = jnp.where(
             idx_ref[...] == lax.broadcasted_iota(jnp.int32, (symbols, positions), 0), 1.0, 0.0
         ).astype(jnp.bfloat16)
-        looked = jnp.dot(em_ref[at, :], one_hot, preferred_element_type=jnp.float32)
-        block = adj_ref[at, :].astype(jnp.float32) * looked
+        looked = jnp.dot(ebuf[b], one_hot, preferred_element_type=jnp.float32)
+        block = abuf[b].astype(jnp.float32) * looked
         w[p * chunks + k] = block.T.astype(jnp.bfloat16)
 
-    own_block(0)
+    own_block(jnp.int32(0))
     pl.semaphore_wait(barrier, jnp.where(p > 0, 1, 0) + jnp.where(p < n - 1, 1, 0) + (m - 1))
 
     def send_own(k, _):
@@ -174,10 +191,6 @@
         b = lax.rem(q, 2)
         return pltpu.make_async_copy(trans_ref.at[:, columns(q)], tbuf.at[b], t_sem.at[b])
 
-    def o_copy(q):
-        b = lax.rem(q, 2)
-        return pltpu.make_async_copy(obuf.at[b], scaled_ref.at[:, columns(q)], o_sem.at[b])
-
     t_copy(0).start()
 
     def block(q, _):
@@ -193,10 +206,6 @@
         def _():
             w_arrive(slot, k)
 
-        @pl.when(q >= 2)
-        def _():
-            o_copy(q - 2).wait()
-
         t_copy(q).wait()
         i = slot * chunks + k
 
@@ -204,7 +213,7 @@
             at = pl.ds(pl.multiple_of(r * ROWS, ROWS), ROWS)
             counts = jnp.dot(f[at, :], w[i], preferred_element_type=jnp.float32)
             scaled = counts * tbuf[b, at, :].astype(jnp.float32)
-            obuf[b, at, :] = scaled.astype(jnp.bfloat16)
+            scaled_ref[at, columns(q)] = scaled.astype(jnp.bfloat16)
             part = scaled[:, :128]
             for g in range(1, CHUNK // 128):
                 part = part + scaled[:, g * 128:(g + 1) * 128]
@@ -212,7 +221,6 @@
             return 0
 
         lax.fori_loop(0, rows // ROWS, tile, 0)
-        o_copy(q).start()
         return 0
 
     lax.fori_loop(0, n * chunks, block, 0)
@@ -231,8 +239,6 @@
 
     for step in range(1, m):
         tot_copy(c, step, lax.rem(c + step, m)).start()
-    o_copy(n * chunks - 2).wait()
-    o_copy(n * chunks - 1).wait()
     for step in range(1, m):
         tot_copy(lax.rem(c + step, m), step, c).wait_recv()
     factor_ref[...] = states / jnp.sum(tot[...], axis=0)
@@ -280,24 +286,25 @@
     scaled, factor = pl.pallas_call(
         functools.partial(kernel, n, m, float(cols * m)),
         out_shape=(
-            jax.ShapeDtypeStruct((rows, cols), jnp.bfloat16),
+            pltpu.VMEM((rows, cols), jnp.bfloat16),
             jax.ShapeDtypeStruct((1, rows), jnp.float32),
         ),
-        in_specs=[vmem, vmem, vmem, anywhere, anywhere],
-        out_specs=(anywhere, vmem),
+        in_specs=[vmem, anywhere, anywhere, anywhere, anywhere],
+        out_specs=(vmem, vmem),
         scratch_shapes=[
             pltpu.VMEM((n * chunks, positions, CHUNK), jnp.bfloat16),
             pltpu.VMEM((rows, positions), jnp.bfloat16),
-            pltpu.VMEM((2, rows, CHUNK), jnp.bfloat16),
+            pltpu.VMEM((2, CHUNK, positions), jnp.bfloat16),
+            pltpu.VMEM((2, CHUNK, emission.shape[1]), jnp.bfloat16),
             pltpu.VMEM((2, rows, CHUNK), jnp.bfloat16),
             pltpu.VMEM((rows, 128), jnp.float32),
             pltpu.VMEM((m, 1, rows), jnp.float32),
             dma((n * chunks,)), dma((n * chunks,)), dma((n * chunks,)),
             dma((m * chunks,)), dma((m * chunks,)), dma((m * chunks,)),
-            dma((2,)), dma((2,)), dma((m,)), dma((m,)), dma,
+            dma((2,)), dma((2,)), dma((2,)), dma((m,)), dma((m,)), dma,
         ],
         compiler_params=pltpu.CompilerParams(
-            collective_id=0, has_side_effects=True, vmem_limit_bytes=48 * 1024 * 1024),
+            collective_id=0, has_side_effects=True, vmem_limit_bytes=29 * 1024 * 1024),
         cost_estimate=pl.CostEstimate(
             flops=2 * rows * cols * positions, bytes_accessed=4 * rows * cols, transcendentals=0),
         name="counts_gather",

time: 181 us -> 189 us (1.044)
  local copies, waits for them, and re-layouts: 4.91 us -> 11.7 us
    unnamed x8 -> x2, local copies, waits for them, and re-layouts: 4.91 us -> 11.7 us
where the time goes in v2:
time: 189 us
  Pallas kernels  154 us (81%)
  other arithmetic  23.1 us (12%)
  local copies, waits for them, and re-layouts  11.7 us (6%)
    pallas_call x1, Pallas kernels, fused(): pl.pallas_call(functools.partial(kernel, n, m, float(cols * m)), out_shap...  154 us
    convert_element_type x1, other arithmetic, fused(): (scaled.astype(jnp.float32) * factor.reshape(rows, 1)).astype(jnp.bfloat16)  23.1 us
    unnamed x2, local copies, waits for them, and re-layouts  11.7 us

profile of v2, /device:TPU:0, one launch (start us, length us, event | category | flops | bytes accessed | tf_op | source)
XLA Modules:
  0.0 188.8 jit_solution(8581987107342267774)
XLA Ops:
  0.0 154.0 %counts_gather.1 = (bf16[4096,4096]{1,0:T(8,128)(2,1)S(1)}, f32[1,4096]{1,0:T(1,128)}) custom-call(s32[1,1024]{1,0:T(1,128)} %bitcast.3, bf16[1024,256]{1,0:T(8,128)(2,1)} %em_ref.1, bf16[1024,1024]{1,0:T(8,128)(2,1)} %adj_ref.1, bf16[1024,1024]{1,0:T(8,128)(2,1)} %fwd_ref.1, bf16[4096,4096]{1,0:T(8,128)(2,1)} %trans_ref.1), custom_call_target="tpu_custom_call" | custom-call | flops 34359738368 | bytes 67108864 | tf_op jit(solution)/shard_map/counts_gather/pallas_call | solution.py:286
  154.0 0.0 copy-start
  154.0 11.7 %copy-done = bf16[4096,4096]{1,0:T(8,128)(2,1)} copy-done((bf16[4096,4096]{1,0:T(8,128)(2,1)}, bf16[4096,4096]{1,0:T(8,128)(2,1)S(1)}, u32[]{:S(2)}) %copy-start) | copy-done | bytes 33554456
  165.7 23.1 %multiply_convert_fusion = bf16[4096,4096]{1,0:T(8,128)(2,1)} fusion(bf16[4096,4096]{1,0:T(8,128)(2,1)} %copy-done, f32[4096]{0:T(1024)} %bitcast.2), kind=kLoop, calls=%fused_computation | loop fusion | flops 50331648 | bytes 67125248 | tf_op jit(solution)/shard_map/convert_element_type | solution.py:312
Async XLA Ops:
  154.0 11.7 %copy-start = (bf16[4096,4096]{1,0:T(8,128)(2,1)}, bf16[4096,4096]{1,0:T(8,128)(2,1)S(1)}, u32[]{:S(2)}) copy-start(bf16[4096,4096]{1,0:T(8,128)(2,1)S(1)} %get-tuple-element.7) | copy-start | bytes 100663296

commit v3 on v2

--- a/solution.py
+++ b/solution.py
@@ -8,15 +8,15 @@
 from jax.sharding import PartitionSpec as P
 
 CHUNK = 256
-ROWS = 512
+ROWS = 1024
 MESH = pl.DeviceIdType.MESH
 
 
 def kernel(n, m, states, idx_ref, em_ref, adj_ref, fwd_ref, trans_ref,
            scaled_ref, factor_ref,
-           w, f, abuf, ebuf, tbuf, acc, tot,
+           w, f, abuf, ebuf, tbuf, obuf, acc, tot,
            w_recv, w_right, w_left, f_recv, f_right, f_left,
-           t_sem, a_sem, e_sem, tot_send, tot_recv, load_sem):
+           a_sem, e_sem, t_sem, o_sem, tot_send, tot_recv, load_sem):
     groups = lax.axis_index("groups")
     p = lax.axis_index("row")
     c = lax.axis_index("col")
@@ -191,6 +191,10 @@
         b = lax.rem(q, 2)
         return pltpu.make_async_copy(trans_ref.at[:, columns(q)], tbuf.at[b], t_sem.at[b])
 
+    def o_copy(q):
+        b = lax.rem(q, 2)
+        return pltpu.make_async_copy(obuf.at[b], scaled_ref.at[:, columns(q)], o_sem.at[b])
+
     t_copy(0).start()
 
     def block(q, _):
@@ -206,6 +210,10 @@
         def _():
             w_arrive(slot, k)
 
+        @pl.when(q >= 2)
+        def _():
+            o_copy(q - 2).wait()
+
         t_copy(q).wait()
         i = slot * chunks + k
 
@@ -213,7 +221,7 @@
             at = pl.ds(pl.multiple_of(r * ROWS, ROWS), ROWS)
             counts = jnp.dot(f[at, :], w[i], preferred_element_type=jnp.float32)
             scaled = counts * tbuf[b, at, :].astype(jnp.float32)
-            scaled_ref[at, columns(q)] = scaled.astype(jnp.bfloat16)
+            obuf[b, at, :] = scaled.astype(jnp.bfloat16)
             part = scaled[:, :128]
             for g in range(1, CHUNK // 128):
                 part = part + scaled[:, g * 128:(g + 1) * 128]
@@ -221,6 +229,7 @@
             return 0
 
         lax.fori_loop(0, rows // ROWS, tile, 0)
+        o_copy(q).start()
         return 0
 
     lax.fori_loop(0, n * chunks, block, 0)
@@ -239,6 +248,8 @@
 
     for step in range(1, m):
         tot_copy(c, step, lax.rem(c + step, m)).start()
+    o_copy(n * chunks - 2).wait()
+    o_copy(n * chunks - 1).wait()
     for step in range(1, m):
         tot_copy(lax.rem(c + step, m), step, c).wait_recv()
     factor_ref[...] = states / jnp.sum(tot[...], axis=0)
@@ -286,25 +297,26 @@
     scaled, factor = pl.pallas_call(
         functools.partial(kernel, n, m, float(cols * m)),
         out_shape=(
-            pltpu.VMEM((rows, cols), jnp.bfloat16),
+            jax.ShapeDtypeStruct((rows, cols), jnp.bfloat16),
             jax.ShapeDtypeStruct((1, rows), jnp.float32),
         ),
         in_specs=[vmem, anywhere, anywhere, anywhere, anywhere],
-        out_specs=(vmem, vmem),
+        out_specs=(anywhere, vmem),
         scratch_shapes=[
             pltpu.VMEM((n * chunks, positions, CHUNK), jnp.bfloat16),
             pltpu.VMEM((rows, positions), jnp.bfloat16),
             pltpu.VMEM((2, CHUNK, positions), jnp.bfloat16),
             pltpu.VMEM((2, CHUNK, emission.shape[1]), jnp.bfloat16),
             pltpu.VMEM((2, rows, CHUNK), jnp.bfloat16),
+            pltpu.VMEM((2, rows, CHUNK), jnp.bfloat16),
             pltpu.VMEM((rows, 128), jnp.float32),
             pltpu.VMEM((m, 1, rows), jnp.float32),
             dma((n * chunks,)), dma((n * chunks,)), dma((n * chunks,)),
             dma((m * chunks,)), dma((m * chunks,)), dma((m * chunks,)),
-            dma((2,)), dma((2,)), dma((2,)), dma((m,)), dma((m,)), dma,
+            dma((2,)), dma((2,)), dma((2,)), dma((2,)), dma((m,)), dma((m,)), dma,
         ],
         compiler_params=pltpu.CompilerParams(
-            collective_id=0, has_side_effects=True, vmem_limit_bytes=29 * 1024 * 1024),
+            collective_id=0, has_side_effects=True, vmem_limit_bytes=60 * 1024 * 1024),
         cost_estimate=pl.CostEstimate(
             flops=2 * rows * cols * positions, bytes_accessed=4 * rows * cols, transcendentals=0),
         name="counts_gather",
@@ -330,7 +342,8 @@
 
     def body(forward, adjoint, emission, emit_index, transition):
         args = (forward, adjoint, emission, emit_index, transition)
-        if n > 2 and m > 1 and forward.shape[0] % CHUNK == 0:
+        tiled = forward.shape[0] % CHUNK == 0 and transition.shape[0] % ROWS == 0
+        if n > 2 and m > 1 and tiled:
             return fused(n, m, *args)
         return plain(m, *args)
 

time: 189 us -> 173 us (0.915)
  local copies, waits for them, and re-layouts: 11.7 us -> 0 us
  Pallas kernels: 154 us -> 150 us
    unnamed x2 -> x0, local copies, waits for them, and re-layouts: 11.7 us -> none
    pallas_call x1, Pallas kernels: 154 us -> 150 us  [fused(): pl.pallas_call(functools.partial(kernel, n, m, float(cols * m)), out_shap...]
where the time goes in v3:
time: 173 us
  Pallas kernels  150 us (87%)
  other arithmetic  23.1 us (13%)
    pallas_call x1, Pallas kernels, fused(): pl.pallas_call(functools.partial(kernel, n, m, float(cols * m)), out_shap...  150 us
    convert_element_type x1, other arithmetic, fused(): (scaled.astype(jnp.float32) * factor.reshape(rows, 1)).astype(jnp.bfloat16)  23.1 us

profile of v3, /device:TPU:0, one launch (start us, length us, event | category | flops | bytes accessed | tf_op | source)
XLA Modules:
  0.0 172.8 jit_solution(17841497102696549262)
XLA Ops:
  0.0 149.7 %counts_gather.1 = (bf16[4096,4096]{1,0:T(8,128)(2,1)}, f32[1,4096]{1,0:T(1,128)}) custom-call(s32[1,1024]{1,0:T(1,128)} %bitcast.3, bf16[1024,256]{1,0:T(8,128)(2,1)} %em_ref.1, bf16[1024,1024]{1,0:T(8,128)(2,1)} %adj_ref.1, bf16[1024,1024]{1,0:T(8,128)(2,1)} %fwd_ref.1, bf16[4096,4096]{1,0:T(8,128)(2,1)} %trans_ref.1), custom_call_target="tpu_custom_call" | custom-call | flops 34359738368 | bytes 67108864 | tf_op jit(solution)/shard_map/counts_gather/pallas_call | solution.py:297
  149.7 23.1 %multiply_convert_fusion = bf16[4096,4096]{1,0:T(8,128)(2,1)} fusion(bf16[4096,4096]{1,0:T(8,128)(2,1)} %get-tuple-element.7, f32[4096]{0:T(1024)} %bitcast.2), kind=kLoop, calls=%fused_computation | loop fusion | flops 50331648 | bytes 67125248 | tf_op jit(solution)/shard_map/convert_element_type | solution.py:324
